TPU v7x, 32 devices: a whole 2x2x4 slice. The times are simulated.
32 devices in a mesh: dp: 8 (over z, x), section: 4 (over y, core).
Axes of the slice: x: 2, y: 2, z: 4, core: 2. Of those that a mesh axis runs over, the one named last changes fastest.
Arguments:
- images_in: bfloat16 [2048, 4096], P(('dp', 'section')), may hold values from -6 to 6
- labels: int32 [2048], P(('dp', 'section')), may hold values from 0 to 9
- conv_weight: float32 [3, 2, 576, 64], P(None, None, None, 'section'), may hold values from -0.25 to 0.25
- frn_gain: float32 [3, 2, 64], replicated, may hold values from 0.25 to 1.75
- frn_bias: float32 [3, 2, 64], replicated, may hold values from -3 to 3
- head_weight: float32 [64, 10], replicated, as said below
- head_bias: float32 [10], replicated, may hold values from -4 to 4
Outputs:
- grad_conv: float32 [3, 2, 576, 64], P(None, None, None, 'section')
- grad_norm: float32 [3, 2, 2, 64], replicated
- grad_head_weight: float32 [64, 10], replicated
- grad_head_bias: float32 [10], replicated
Inputs may be any that keep to these rules, and one draw needn't show every extreme that they name: `head_weight`: the classifier's weights.
All inputs are finite; a program needn't handle non-finite values.
Results may differ from a plain program's by a relative error of at most 0.0033.
The roundings to bfloat16 on the way count: a program that leaves them out, or rounds other values in their place, can miss the bound.
Values may be sent and summed in bfloat16 or wider, within the bound.
A program may use at most 64 MiB of HBM per device.

v0:
```python
import jax
import jax.numpy as jnp
from jax import lax
from jax.sharding import PartitionSpec as P

SIDE = 8
MICRO = 8
eps = 1e-06
prior_precision = 0.5


def make_patches(maps):
    side = maps.shape[1]
    padded = jnp.pad(maps, ((0, 0), (1, 1), (1, 1), (0, 0)))
    taps = [padded[:, a : a + side, e : e + side, :] for a in range(3) for e in range(3)]
    stacked = jnp.concatenate(taps, axis=3)
    return stacked.reshape(maps.shape[0] * side * side, 9 * maps.shape[3])


def fold_patches(columns, shape):
    back = jax.vjp(make_patches, jnp.zeros(shape, jnp.float32))[1]
    return back(columns)[0]


def respond(values, gain, bias, count):
    grouped = values.reshape(count, -1, values.shape[1])
    energy = jnp.mean(grouped * grouped, axis=1, keepdims=True)
    normed = grouped * lax.rsqrt(energy + eps)
    return (gain * normed + bias).reshape(values.shape)


def swish(values):
    return values * jax.nn.sigmoid(values)


def block_forward(maps, weights, gains, biases):
    count = maps.shape[0]
    w_first = weights[0]
    w_second = weights[1]
    cols_first = make_patches(maps)
    pre_first = jnp.dot(cols_first, w_first, preferred_element_type=jnp.float32)
    hidden = swish(respond(pre_first, gains[0], biases[0], count)).astype(jnp.bfloat16)
    cols_second = make_patches(hidden.reshape(maps.shape))
    pre_second = jnp.dot(cols_second, w_second, preferred_element_type=jnp.float32)
    skip = maps.reshape(pre_second.shape).astype(jnp.float32)
    result = swish(skip + respond(pre_second, gains[1], biases[1], count)).astype(jnp.bfloat16)
    return (result.reshape(maps.shape), (cols_first, pre_first, cols_second, pre_second))


def block_backward(maps, cotangent, weights, gains, biases):
    count = maps.shape[0]
    w_first = weights[0]
    w_second = weights[1]
    saved = block_forward(maps, weights, gains, biases)[1]
    cols_first, pre_first, cols_second, pre_second = saved

    def second_part(values, skip, gain, bias):
        return swish(skip + respond(values, gain, bias, count))

    def first_part(values, gain, bias):
        return swish(respond(values, gain, bias, count))

    skip = maps.reshape(pre_second.shape).astype(jnp.float32)
    back_second = jax.vjp(second_part, pre_second, skip, gains[1], biases[1])[1]
    d_second, d_skip, dg_second, db_second = back_second(
        cotangent.reshape(pre_second.shape).astype(jnp.float32)
    )
    q_second = d_second.astype(jnp.bfloat16)
    dw_second = jnp.dot(cols_second.T, q_second, preferred_element_type=jnp.float32)
    d_hidden = fold_patches(
        jnp.dot(q_second, w_second.T, preferred_element_type=jnp.float32), maps.shape
    )
    back_first = jax.vjp(first_part, pre_first, gains[0], biases[0])[1]
    d_first, dg_first, db_first = back_first(d_hidden.reshape(pre_first.shape))
    q_first = d_first.astype(jnp.bfloat16)
    dw_first = jnp.dot(cols_first.T, q_first, preferred_element_type=jnp.float32)
    d_input = fold_patches(
        jnp.dot(q_first, w_first.T, preferred_element_type=jnp.float32), maps.shape
    )
    d_maps = (d_skip.reshape(maps.shape) + d_input).astype(jnp.bfloat16)
    d_norm = jnp.stack([jnp.stack([dg_first, db_first]), jnp.stack([dg_second, db_second])])
    return (d_maps, jnp.stack([dw_first, dw_second]), d_norm)


def head_grads(final, labels, head_w, head_b, total):
    count = final.shape[0]
    width = final.shape[3]
    pixels = final.shape[1] * final.shape[2]
    pooled = jnp.mean(final.reshape(count, pixels, width).astype(jnp.float32), axis=1)
    logits = jnp.dot(pooled, head_w, precision=lax.Precision.HIGHEST) + head_b
    top = jnp.max(logits, axis=1, keepdims=True)
    expo = jnp.exp(logits - top)
    probs = expo / jnp.sum(expo, axis=1, keepdims=True)
    onehot = (labels[:, None] == jnp.arange(head_w.shape[1])[None, :]).astype(jnp.float32)
    d_logits = (probs - onehot) / total
    d_head_w = jnp.dot(pooled.T, d_logits, precision=lax.Precision.HIGHEST)
    d_head_b = jnp.sum(d_logits, axis=0)
    d_pooled = jnp.dot(d_logits, head_w.T, precision=lax.Precision.HIGHEST) / pixels
    spread = jnp.broadcast_to(d_pooled[:, None, :], (count, pixels, width))
    return (spread.astype(jnp.bfloat16).reshape(final.shape), d_head_w, d_head_b)


def group_grads(maps, labels, weights, gains, biases, head_w, head_b, total):
    saved = []
    for index in range(weights.shape[0]):
        saved.append(maps)
        maps = block_forward(maps, weights[index], gains[index], biases[index])[0]
    cotangent, d_head_w, d_head_b = head_grads(maps, labels, head_w, head_b, total)
    conv_terms = []
    norm_terms = []
    for index in reversed(range(weights.shape[0])):
        cotangent, d_conv, d_norm = block_backward(
            saved[index], cotangent, weights[index], gains[index], biases[index]
        )
        conv_terms.insert(0, d_conv)
        norm_terms.insert(0, d_norm)
    return (jnp.stack(conv_terms), jnp.stack(norm_terms), d_head_w, d_head_b)


def accumulate(maps, labels, weights, gains, biases, head_w, head_b, total):
    width = weights.shape[3]
    initial = (
        jnp.zeros(weights.shape, jnp.float32),
        jnp.zeros((weights.shape[0], 2, 2, width), jnp.float32),
        jnp.zeros(head_w.shape, jnp.float32),
        jnp.zeros(head_b.shape, jnp.float32),
    )

    def advance(carry, item):
        terms = group_grads(item[0], item[1], weights, gains, biases, head_w, head_b, total)
        return (tuple((left + right for left, right in zip(carry, terms))), None)

    return lax.scan(advance, initial, (maps, labels))[0]


def per_device(images_in, labels, conv_weight, frn_gain, frn_bias, head_weight, head_bias):
    images = images_in.shape[0]
    width = frn_gain.shape[2]
    share = conv_weight.shape[3]
    total = images * lax.axis_size("dp") * lax.axis_size("section")
    offset = lax.axis_index("section") * share
    rounded_share = conv_weight.astype(jnp.bfloat16)
    all_conv = lax.all_gather(rounded_share, "section", axis=3, tiled=True)
    group_size = images // MICRO
    maps = images_in.reshape(MICRO, group_size, SIDE, SIDE, width)
    label_groups = labels.reshape(MICRO, group_size)
    conv_grad, norm_grad, head_w_grad, head_b_grad = accumulate(
        maps, label_groups, all_conv, frn_gain, frn_bias, head_weight, head_bias, total
    )
    summed = lax.psum(conv_grad, ("dp", "section"))
    conv_owned = lax.dynamic_slice_in_dim(summed, offset, share, 3)
    norm_sum, head_w_sum, head_b_sum = lax.psum(
        (norm_grad, head_w_grad, head_b_grad), ("dp", "section")
    )
    params = jnp.stack([frn_gain, frn_bias], axis=2)
    return (
        conv_owned + prior_precision * conv_weight,
        norm_sum + prior_precision * params,
        head_w_sum + prior_precision * head_weight,
        head_b_sum + prior_precision * head_bias,
    )


def solution(mesh):
    return jax.shard_map(
        per_device,
        mesh=mesh,
        in_specs=(
            P(("dp", "section"), None),
            P(("dp", "section")),
            P(None, None, None, "section"),
            P(),
            P(),
            P(),
            P(),
        ),
        out_specs=(P(None, None, None, "section"), P(), P(), P()),
        check_vma=False,
    )
```

profile of v0, /device:TPU:0, one launch (start us, length us, event | category | flops | bytes accessed | tf_op | source)
XLA Modules:
  0.0 816.5 jit_solution(12413973247500979296)
XLA Ops:
  9.6 8.5 %all_gather.3 = bf16[3,2,576,64]{2,3,1,0:T(8,128)(2,1)S(1)} all-gather(bf16[3,2,576,16]{2,3,1,0:T(8,128)(2,1)S(1)} %convert_element_type.386), channel_id=1, replica_groups=mesh['dp'=8,'section'=4] {'section'}, dimensions={3}, use_global_device_ids=true | all-gather | bytes 552960 | tf_op jit(solution)/shard_map/all_gather | solution.py:143
  19.2 659.0 %while.19 = (s32[]{:T(128)}, f32[3,2,576,64]{2,3,1,0:T(8,128)}, f32[3,2,2,64]{3,2,1,0:T(2,128)}, f32[64,10]{0,1:T(8,128)}, f32[10]{0:T(128)}, /*index=5*/bf16[8,...) while((s32[]{:T(128)}, f32[3,2,576,64]{2,3,1,0:T(8,128)}, ...), condition=%wide.region_29.30_spmd.clone, body=%wide.region_0.29_spmd.clone.sunk | while | flops 655682368 | bytes 99941760 | solution.py:133
  27.5 3.8 pad_slice_fusion.54
  37.1 4.0 pad_slice_fusion.55
  56.0 4.0 pad_slice_fusion.57
  69.6 4.0 fusion.302
  73.6 2.2 concatenate.404
  109.9 3.8 pad_slice_fusion.54
  119.4 4.0 pad_slice_fusion.55
  138.3 4.0 pad_slice_fusion.57
  152.0 4.0 fusion.302
  156.0 2.2 concatenate.404
  158.2 2.2 concatenate.405
  192.2 3.8 pad_slice_fusion.54
  201.8 4.0 pad_slice_fusion.55
  220.7 4.0 pad_slice_fusion.57
  234.3 4.0 fusion.302
  238.3 2.2 concatenate.404
  274.6 3.8 pad_slice_fusion.54
  284.2 4.0 pad_slice_fusion.55
  303.1 4.0 pad_slice_fusion.57
  316.7 4.0 fusion.302
  320.7 2.2 concatenate.404
  356.9 3.8 pad_slice_fusion.54
  366.5 4.0 pad_slice_fusion.55
  385.4 4.0 pad_slice_fusion.57
  399.1 4.0 fusion.302
  403.1 2.2 concatenate.404
  405.3 2.2 concatenate.405
  439.3 3.8 pad_slice_fusion.54
  448.9 4.0 pad_slice_fusion.55
  467.8 4.0 pad_slice_fusion.57
  481.4 4.0 fusion.302
  485.4 2.2 concatenate.404
  487.6 2.2 concatenate.405
  521.7 3.8 pad_slice_fusion.54
  531.3 4.0 pad_slice_fusion.55
  550.2 4.0 pad_slice_fusion.57
  563.8 4.0 fusion.302
  567.8 2.2 concatenate.404
  570.0 2.2 concatenate.405
  604.0 3.8 pad_slice_fusion.54
  613.6 4.0 pad_slice_fusion.55
  632.5 4.0 pad_slice_fusion.57
  646.1 4.0 fusion.302
  650.2 2.2 concatenate.404
  678.2 40.8 %all-reduce.51 = (f32[3,2,2,64]{3,2,1,0:T(2,128)S(1)}, f32[64,10]{0,1:T(8,128)S(1)}, f32[10]{0:T(128)S(1)}) all-reduce(f32[3,2,2,64]{3,2,1,0:T(2,128)} %get-tuple-element.157, f32[64,10]{0,1:T(8,128)} %get-tuple-element.158, f32[10]{0:T(128)} %get-tuple-element.159), channel_id=1, replica_groups=mesh['dp'=8,'section'=4] {'dp','section'}, use_global_device_ids=true, to_apply=%region_31.32 | all-reduce | flops 1418 | bytes 11344 | tf_op jit(solution)/shard_map/psum | solution.py:152
  722.8 85.1 %all-reduce.54.cloned.1.call-done = f32[3,2,576,64]{2,3,1,0:T(8,128)} async-done(((f32[3,2,576,64]{2,3,1,0:T(8,128)}), f32[3,2,576,64]{2,3,1,0:T(8,128)}) %all-reduce.54.cloned.1.call-update) | async-done | bytes 884752 | tf_op jit(solution)/shard_map/psum | solution.py:150
  (1643 shorter events, 508.5 us)
Async XLA Ops:
  7.2 10.9 %copy-start.31 = (bf16[64,4096]{1,0:T(8,128)(2,1)S(1)}, bf16[64,4096]{1,0:T(8,128)(2,1)}, u32[]{:S(2)}) copy-start(bf16[64,4096]{1,0:T(8,128)(2,1)} %param.9) | copy-start | bytes 1572868
  7.2 800.7 %all-reduce.54.cloned.1.call-start = ((), (), s32[]{:S(2)}) async-start(), calls=%async_computation | async-start | bytes 1966080 | tf_op jit(solution)/shard_map/psum | solution.py:150
  19.2 4.6 copy-start.7
  19.2 23.2 %copy-start.5 = (bf16[3,2,576,64]{2,3,1,0:T(8,128)(2,1)}, bf16[3,2,576,64]{2,3,1,0:T(8,128)(2,1)S(1)}, u32[]{:S(2)}) copy-start(bf16[3,2,576,64]{2,3,1,0:T(8,128)(2,1)S(1)} %get-tuple-element.949) | copy-start | bytes 1327108 | tf_op jit(solution)/shard_map/while
  21.9 11.3 %copy-start.43 = (f32[64]{0:T(128)}, f32[64]{0:T(128)S(1)}, u32[]{:S(2)}) copy-start(f32[64]{0:T(128)S(1)} %get-tuple-element.737) | copy-start | bytes 772 | tf_op jit(solution)/shard_map/while
  21.9 20.9 %copy-start.40 = (f32[64]{0:T(128)}, f32[64]{0:T(128)S(1)}, u32[]{:S(2)}) copy-start(f32[64]{0:T(128)S(1)} %get-tuple-element.752) | copy-start | bytes 772 | tf_op jit(solution)/shard_map/while
  21.9 5.1 copy-start.11
  101.6 4.6 copy-start.7
  101.6 23.1 %copy-start.5 = (bf16[3,2,576,64]{2,3,1,0:T(8,128)(2,1)}, bf16[3,2,576,64]{2,3,1,0:T(8,128)(2,1)S(1)}, u32[]{:S(2)}) copy-start(bf16[3,2,576,64]{2,3,1,0:T(8,128)(2,1)S(1)} %get-tuple-element.949) | copy-start | bytes 1327108 | tf_op jit(solution)/shard_map/while
  104.2 11.3 %copy-start.43 = (f32[64]{0:T(128)}, f32[64]{0:T(128)S(1)}, u32[]{:S(2)}) copy-start(f32[64]{0:T(128)S(1)} %get-tuple-element.737) | copy-start | bytes 772 | tf_op jit(solution)/shard_map/while
  104.2 20.9 %copy-start.40 = (f32[64]{0:T(128)}, f32[64]{0:T(128)S(1)}, u32[]{:S(2)}) copy-start(f32[64]{0:T(128)S(1)} %get-tuple-element.752) | copy-start | bytes 772 | tf_op jit(solution)/shard_map/while
  104.3 5.1 copy-start.11
  128.8 4.3 copy-start.12
  184.0 4.6 copy-start.7
  184.0 23.1 %copy-start.5 = (bf16[3,2,576,64]{2,3,1,0:T(8,128)(2,1)}, bf16[3,2,576,64]{2,3,1,0:T(8,128)(2,1)S(1)}, u32[]{:S(2)}) copy-start(bf16[3,2,576,64]{2,3,1,0:T(8,128)(2,1)S(1)} %get-tuple-element.949) | copy-start | bytes 1327108 | tf_op jit(solution)/shard_map/while
  186.6 11.3 %copy-start.43 = (f32[64]{0:T(128)}, f32[64]{0:T(128)S(1)}, u32[]{:S(2)}) copy-start(f32[64]{0:T(128)S(1)} %get-tuple-element.737) | copy-start | bytes 772 | tf_op jit(solution)/shard_map/while
  186.6 20.9 %copy-start.40 = (f32[64]{0:T(128)}, f32[64]{0:T(128)S(1)}, u32[]{:S(2)}) copy-start(f32[64]{0:T(128)S(1)} %get-tuple-element.752) | copy-start | bytes 772 | tf_op jit(solution)/shard_map/while
  186.6 5.1 copy-start.11
  211.2 4.3 copy-start.12
  266.3 4.6 copy-start.7
  266.3 23.1 %copy-start.5 = (bf16[3,2,576,64]{2,3,1,0:T(8,128)(2,1)}, bf16[3,2,576,64]{2,3,1,0:T(8,128)(2,1)S(1)}, u32[]{:S(2)}) copy-start(bf16[3,2,576,64]{2,3,1,0:T(8,128)(2,1)S(1)} %get-tuple-element.949) | copy-start | bytes 1327108 | tf_op jit(solution)/shard_map/while
  268.9 11.3 %copy-start.43 = (f32[64]{0:T(128)}, f32[64]{0:T(128)S(1)}, u32[]{:S(2)}) copy-start(f32[64]{0:T(128)S(1)} %get-tuple-element.737) | copy-start | bytes 772 | tf_op jit(solution)/shard_map/while
  269.0 20.9 %copy-start.40 = (f32[64]{0:T(128)}, f32[64]{0:T(128)S(1)}, u32[]{:S(2)}) copy-start(f32[64]{0:T(128)S(1)} %get-tuple-element.752) | copy-start | bytes 772 | tf_op jit(solution)/shard_map/while
  269.0 5.1 copy-start.11
  293.5 4.3 copy-start.12
  348.7 4.6 copy-start.7
  348.7 23.1 %copy-start.5 = (bf16[3,2,576,64]{2,3,1,0:T(8,128)(2,1)}, bf16[3,2,576,64]{2,3,1,0:T(8,128)(2,1)S(1)}, u32[]{:S(2)}) copy-start(bf16[3,2,576,64]{2,3,1,0:T(8,128)(2,1)S(1)} %get-tuple-element.949) | copy-start | bytes 1327108 | tf_op jit(solution)/shard_map/while
  351.3 11.3 %copy-start.43 = (f32[64]{0:T(128)}, f32[64]{0:T(128)S(1)}, u32[]{:S(2)}) copy-start(f32[64]{0:T(128)S(1)} %get-tuple-element.737) | copy-start | bytes 772 | tf_op jit(solution)/shard_map/while
  351.3 20.9 %copy-start.40 = (f32[64]{0:T(128)}, f32[64]{0:T(128)S(1)}, u32[]{:S(2)}) copy-start(f32[64]{0:T(128)S(1)} %get-tuple-element.752) | copy-start | bytes 772 | tf_op jit(solution)/shard_map/while
  351.4 5.1 copy-start.11
  375.9 4.3 copy-start.12
  431.1 4.6 copy-start.7
  431.1 23.1 %copy-start.5 = (bf16[3,2,576,64]{2,3,1,0:T(8,128)(2,1)}, bf16[3,2,576,64]{2,3,1,0:T(8,128)(2,1)S(1)}, u32[]{:S(2)}) copy-start(bf16[3,2,576,64]{2,3,1,0:T(8,128)(2,1)S(1)} %get-tuple-element.949) | copy-start | bytes 1327108 | tf_op jit(solution)/shard_map/while
  433.7 11.3 %copy-start.43 = (f32[64]{0:T(128)}, f32[64]{0:T(128)S(1)}, u32[]{:S(2)}) copy-start(f32[64]{0:T(128)S(1)} %get-tuple-element.737) | copy-start | bytes 772 | tf_op jit(solution)/shard_map/while
  433.7 20.9 %copy-start.40 = (f32[64]{0:T(128)}, f32[64]{0:T(128)S(1)}, u32[]{:S(2)}) copy-start(f32[64]{0:T(128)S(1)} %get-tuple-element.752) | copy-start | bytes 772 | tf_op jit(solution)/shard_map/while
  433.7 5.1 copy-start.11
  458.3 4.3 copy-start.12
  513.4 4.6 copy-start.7
  513.4 23.1 %copy-start.5 = (bf16[3,2,576,64]{2,3,1,0:T(8,128)(2,1)}, bf16[3,2,576,64]{2,3,1,0:T(8,128)(2,1)S(1)}, u32[]{:S(2)}) copy-start(bf16[3,2,576,64]{2,3,1,0:T(8,128)(2,1)S(1)} %get-tuple-element.949) | copy-start | bytes 1327108 | tf_op jit(solution)/shard_map/while
  516.0 11.3 %copy-start.43 = (f32[64]{0:T(128)}, f32[64]{0:T(128)S(1)}, u32[]{:S(2)}) copy-start(f32[64]{0:T(128)S(1)} %get-tuple-element.737) | copy-start | bytes 772 | tf_op jit(solution)/shard_map/while
  516.1 20.9 %copy-start.40 = (f32[64]{0:T(128)}, f32[64]{0:T(128)S(1)}, u32[]{:S(2)}) copy-start(f32[64]{0:T(128)S(1)} %get-tuple-element.752) | copy-start | bytes 772 | tf_op jit(solution)/shard_map/while
  516.1 5.1 copy-start.11
  540.6 4.3 copy-start.12
  595.8 4.6 copy-start.7
  595.8 23.1 %copy-start.5 = (bf16[3,2,576,64]{2,3,1,0:T(8,128)(2,1)}, bf16[3,2,576,64]{2,3,1,0:T(8,128)(2,1)S(1)}, u32[]{:S(2)}) copy-start(bf16[3,2,576,64]{2,3,1,0:T(8,128)(2,1)S(1)} %get-tuple-element.949) | copy-start | bytes 1327108 | tf_op jit(solution)/shard_map/while
  598.4 11.3 %copy-start.43 = (f32[64]{0:T(128)}, f32[64]{0:T(128)S(1)}, u32[]{:S(2)}) copy-start(f32[64]{0:T(128)S(1)} %get-tuple-element.737) | copy-start | bytes 772 | tf_op jit(solution)/shard_map/while
  598.4 20.9 %copy-start.40 = (f32[64]{0:T(128)}, f32[64]{0:T(128)S(1)}, u32[]{:S(2)}) copy-start(f32[64]{0:T(128)S(1)} %get-tuple-element.752) | copy-start | bytes 772 | tf_op jit(solution)/shard_map/while
  598.5 5.1 copy-start.11
  (354 other events, 664.6 us)
Sparse Core Ops, SparseCore 0:
  678.3 129.5 all-reduce.53
where the time goes:
time: 827 us; the launch traced here: 817 us
  local copies, waits for them, and re-layouts  424 us (51%)
  other arithmetic  151 us (18%)
  matrix products  85.6 us (10%)
  waiting for transfers between devices  85.1 us (10%)
  blocking collectives  49.3 us (6%)
  between operations  14.1 us (2%)
    concatenate x104, local copies, waits for them, and re-layouts, make_patches(): stacked = jnp.concatenate(taps, axis=3)  192 us
    slice x40, local copies, waits for them, and re-layouts, make_patches(): padded[:, a:a + side, e:e + side, :]  115 us
    psum x1, waiting for transfers between devices, per_device(): summed = lax.psum(conv_grad, ('dp', 'section'))  85.1 us
    while x800, local copies, waits for them, and re-layouts  72.5 us
    convert_element_type x40, other arithmetic, block_forward(): swish(skip + respond(pre_second, gains[1], biases[1], count))  48.6 us
    psum x1, blocking collectives, per_device(): lax.psum((norm_grad, head_w_grad, head_b_grad), ('dp', 'section'))  40.8 us
    convert_element_type x72, other arithmetic, block_forward(): swish(respond(pre_first, gains[0], biases[0], count)).astype(jnp.bfloat16)  37.2 us
    reduce_sum x48, other arithmetic, respond(): return (gain * normed + bias).reshape(values.shape)  36.8 us
  transfers between devices with their start and end apart: 1, of which 1 were waited for; matrix products, arithmetic and copies ran while one was open for 0% of the time, Pallas kernels for 0%

commit v1 on v0

--- a/solution.py
+++ b/solution.py
@@ -2,6 +2,7 @@
 import jax.numpy as jnp
 from jax import lax
 from jax.sharding import PartitionSpec as P
+from jax.lax import psum
 
 SIDE = 8
 MICRO = 8
@@ -147,7 +148,12 @@
     conv_grad, norm_grad, head_w_grad, head_b_grad = accumulate(
         maps, label_groups, all_conv, frn_gain, frn_bias, head_weight, head_bias, total
     )
-    summed = lax.psum(conv_grad, ("dp", "section"))
+
+    def part_pools_on_mesh(across, state, mesh_name):
+        q_next = psum(psum(state, across), mesh_name)
+        return q_next
+
+    summed = part_pools_on_mesh("section", conv_grad, "dp")
     conv_owned = lax.dynamic_slice_in_dim(summed, offset, share, 3)
     norm_sum, head_w_sum, head_b_sum = lax.psum(
         (norm_grad, head_w_grad, head_b_grad), ("dp", "section")

time: 827 us -> 798 us (0.965)
  local copies, waits for them, and re-layouts: 424 us -> 404 us
  waiting for transfers between devices: 85.1 us -> 75.5 us
    slice x40, local copies, waits for them, and re-layouts: 115 us -> 100 us  [make_patches(): padded[:, a:a + side, e:e + side, :]]
    psum x1 -> x2, waiting for transfers between devices: 85.1 us -> 75.4 us  [part_pools_on_mesh(): q_next = psum(psum(state, across), mesh_name)]
    while x800 -> x928, local copies, waits for them, and re-layouts: 72.5 us -> 66.9 us
  transfers between devices with their start and end apart: 1 -> 2, of which waited for: 1 -> 2; matrix products, arithmetic and copies ran while one was open for 0% -> 0% of each run, Pallas kernels for 0% -> 0%
where the time goes in v1:
time: 798 us; the launch traced here: 788 us
  local copies, waits for them, and re-layouts  404 us (51%)
  other arithmetic  145 us (18%)
  matrix products  92.7 us (12%)
  waiting for transfers between devices  75.5 us (9%)
  blocking collectives  49 us (6%)
  between operations  14.2 us (2%)
    concatenate x104, local copies, waits for them, and re-layouts, make_patches(): stacked = jnp.concatenate(taps, axis=3)  198 us
    slice x40, local copies, waits for them, and re-layouts, make_patches(): padded[:, a:a + side, e:e + side, :]  100 us
    psum x2, waiting for transfers between devices, part_pools_on_mesh(): q_next = psum(psum(state, across), mesh_name)  75.4 us
    while x928, local copies, waits for them, and re-layouts  66.9 us
    convert_element_type x40, other arithmetic, block_forward(): swish(skip + respond(pre_second, gains[1], biases[1], count))  48.9 us
    psum x1, blocking collectives, per_device(): lax.psum((norm_grad, head_w_grad, head_b_grad), ('dp', 'section'))  40.5 us
    reduce_sum x48, other arithmetic, respond(): return (gain * normed + bias).reshape(values.shape)  36.8 us
    convert_element_type x72, other arithmetic, block_forward(): swish(respond(pre_first, gains[0], biases[0], count)).astype(jnp.bfloat16)  32.2 us
  transfers between devices with their start and end apart: 2, of which 2 were waited for; matrix products, arithmetic and copies ran while one was open for 0% of the time, Pallas kernels for 0%

profile of v1, /device:TPU:0, one launch (start us, length us, event | category | flops | bytes accessed | tf_op | source)
XLA Modules:
  0.0 788.0 jit_solution(11380797013124830302)
XLA Ops:
  9.0 8.5 %all_gather.3 = bf16[3,2,576,64]{2,3,1,0:T(8,128)(2,1)S(1)} all-gather(bf16[3,2,576,16]{2,3,1,0:T(8,128)(2,1)S(1)} %convert_element_type.386), channel_id=1, replica_groups=mesh['dp'=8,'section'=4] {'section'}, dimensions={3}, use_global_device_ids=true | all-gather | bytes 552960 | tf_op jit(solution)/shard_map/all_gather | solution.py:144
  18.6 642.3 %while.19 = (s32[]{:T(128)}, f32[3,2,576,64]{2,3,1,0:T(8,128)}, f32[3,2,2,64]{3,2,1,0:T(2,128)}, f32[64,10]{0,1:T(8,128)}, f32[10]{0:T(128)}, /*index=5*/bf16[8,...) while((s32[]{:T(128)}, f32[3,2,576,64]{2,3,1,0:T(8,128)}, ...), condition=%wide.region_29.30_spmd.clone, body=%wide.region_0.29_spmd.clone.sunk | while | flops 655682368 | bytes 101451392 | solution.py:134
  32.6 4.5 pad_slice_fusion.55
  49.9 2.2 concatenate.407
  52.1 4.0 pad_slice_fusion.57
  63.6 2.2 concatenate.406
  65.8 4.7 fusion.302
  70.5 2.2 concatenate.404
  112.9 4.5 pad_slice_fusion.55
  130.2 2.2 concatenate.407
  132.4 4.0 pad_slice_fusion.57
  143.9 2.2 concatenate.406
  146.1 4.7 fusion.302
  150.8 2.2 concatenate.404
  193.2 4.5 pad_slice_fusion.55
  210.5 2.2 concatenate.407
  212.7 4.0 pad_slice_fusion.57
  226.4 4.7 fusion.302
  231.0 2.2 concatenate.404
  273.5 4.5 pad_slice_fusion.55
  290.8 2.2 concatenate.407
  293.0 4.0 pad_slice_fusion.57
  306.6 4.7 fusion.302
  311.3 2.2 concatenate.404
  353.8 4.5 pad_slice_fusion.55
  371.0 2.2 concatenate.407
  373.3 4.0 pad_slice_fusion.57
  386.9 4.7 fusion.302
  391.6 2.2 concatenate.404
  434.1 4.5 pad_slice_fusion.55
  451.3 2.2 concatenate.407
  453.6 4.0 pad_slice_fusion.57
  467.2 4.7 fusion.302
  471.9 2.2 concatenate.404
  514.4 4.5 pad_slice_fusion.55
  531.6 2.2 concatenate.407
  533.8 4.0 pad_slice_fusion.57
  545.3 2.2 concatenate.406
  547.5 4.7 fusion.302
  552.2 2.2 concatenate.404
  594.7 4.5 pad_slice_fusion.55
  611.9 2.2 concatenate.407
  614.1 4.0 pad_slice_fusion.57
  627.8 4.7 fusion.302
  632.5 2.2 concatenate.404
  661.1 36.6 %all-reduce.55.cloned.1.call-done = f32[3,2,576,64]{2,3,1,0:T(8,128)} async-done(((f32[3,2,576,64]{2,3,1,0:T(8,128)}), f32[3,2,576,64]{2,3,1,0:T(8,128)}) %all-reduce.55.cloned.1.call-update) | async-done | bytes 884752 | tf_op jit(solution)/shard_map/psum | solution.py:153
  697.7 40.5 %all-reduce.51 = (f32[3,2,2,64]{3,2,1,0:T(2,128)S(1)}, f32[64,10]{0,1:T(8,128)S(1)}, f32[10]{0:T(128)S(1)}) all-reduce(f32[3,2,2,64]{3,2,1,0:T(2,128)S(1)} %copy-done.45, f32[64,10]{0,1:T(8,128)S(1)} %copy-done.62, f32[10]{0:T(128)S(1)} %copy-done.56), channel_id=1, replica_groups=mesh['dp'=8,'section'=4] {'dp','section'}, use_global_device_ids=true, to_apply=%region_32.33 | all-reduce | flops 1418 | bytes 11344 | tf_op jit(solution)/shard_map/psum | solution.py:158
  740.7 38.8 %all-reduce.57.cloned.1.call-done = f32[3,2,576,64]{2,3,1,0:T(8,128)} async-done(((f32[3,2,576,64]{2,3,1,0:T(8,128)}), f32[3,2,576,64]{2,3,1,0:T(8,128)}) %all-reduce.57.cloned.1.call-update) | async-done | bytes 884752 | tf_op jit(solution)/shard_map/psum | solution.py:153
  (1786 shorter events, 494.2 us)
Async XLA Ops:
  7.2 10.3 %copy-start.38 = (bf16[64,4096]{1,0:T(8,128)(2,1)S(1)}, bf16[64,4096]{1,0:T(8,128)(2,1)}, u32[]{:S(2)}) copy-start(bf16[64,4096]{1,0:T(8,128)(2,1)} %param.9) | copy-start | bytes 1572868
  7.2 690.5 %all-reduce.55.cloned.1.call-start = ((), (), s32[]{:S(2)}) async-start(), calls=%async_computation | async-start | bytes 1966080 | tf_op jit(solution)/shard_map/psum | solution.py:153
  18.6 19.9 %copy-start.5 = (bf16[3,2,576,64]{2,3,1,0:T(8,128)(2,1)}, bf16[3,2,576,64]{2,3,1,0:T(8,128)(2,1)S(1)}, u32[]{:S(2)}) copy-start(bf16[3,2,576,64]{2,3,1,0:T(8,128)(2,1)S(1)} %get-tuple-element.949) | copy-start | bytes 1327108 | tf_op jit(solution)/shard_map/while
  20.6 8.1 %copy-start.52 = (f32[64]{0:T(128)}, f32[64]{0:T(128)S(1)}, u32[]{:S(2)}) copy-start(f32[64]{0:T(128)S(1)} %get-tuple-element.737) | copy-start | bytes 772 | tf_op jit(solution)/shard_map/while
  20.6 18.3 %copy-start.49 = (f32[64]{0:T(128)}, f32[64]{0:T(128)S(1)}, u32[]{:S(2)}) copy-start(f32[64]{0:T(128)S(1)} %get-tuple-element.752) | copy-start | bytes 772 | tf_op jit(solution)/shard_map/while
  20.6 4.1 copy-start.11
  28.6 4.1 copy-start.30
  42.6 4.3 copy-start.12
  98.9 19.9 %copy-start.5 = (bf16[3,2,576,64]{2,3,1,0:T(8,128)(2,1)}, bf16[3,2,576,64]{2,3,1,0:T(8,128)(2,1)S(1)}, u32[]{:S(2)}) copy-start(bf16[3,2,576,64]{2,3,1,0:T(8,128)(2,1)S(1)} %get-tuple-element.949) | copy-start | bytes 1327108 | tf_op jit(solution)/shard_map/while
  100.9 8.1 %copy-start.52 = (f32[64]{0:T(128)}, f32[64]{0:T(128)S(1)}, u32[]{:S(2)}) copy-start(f32[64]{0:T(128)S(1)} %get-tuple-element.737) | copy-start | bytes 772 | tf_op jit(solution)/shard_map/while
  100.9 18.3 %copy-start.49 = (f32[64]{0:T(128)}, f32[64]{0:T(128)S(1)}, u32[]{:S(2)}) copy-start(f32[64]{0:T(128)S(1)} %get-tuple-element.752) | copy-start | bytes 772 | tf_op jit(solution)/shard_map/while
  108.9 4.1 copy-start.30
  122.9 4.3 copy-start.12
  179.2 19.9 %copy-start.5 = (bf16[3,2,576,64]{2,3,1,0:T(8,128)(2,1)}, bf16[3,2,576,64]{2,3,1,0:T(8,128)(2,1)S(1)}, u32[]{:S(2)}) copy-start(bf16[3,2,576,64]{2,3,1,0:T(8,128)(2,1)S(1)} %get-tuple-element.949) | copy-start | bytes 1327108 | tf_op jit(solution)/shard_map/while
  181.2 8.1 %copy-start.52 = (f32[64]{0:T(128)}, f32[64]{0:T(128)S(1)}, u32[]{:S(2)}) copy-start(f32[64]{0:T(128)S(1)} %get-tuple-element.737) | copy-start | bytes 772 | tf_op jit(solution)/shard_map/while
  181.2 18.3 %copy-start.49 = (f32[64]{0:T(128)}, f32[64]{0:T(128)S(1)}, u32[]{:S(2)}) copy-start(f32[64]{0:T(128)S(1)} %get-tuple-element.752) | copy-start | bytes 772 | tf_op jit(solution)/shard_map/while
  189.2 4.1 copy-start.30
  203.2 4.3 copy-start.12
  259.5 19.9 %copy-start.5 = (bf16[3,2,576,64]{2,3,1,0:T(8,128)(2,1)}, bf16[3,2,576,64]{2,3,1,0:T(8,128)(2,1)S(1)}, u32[]{:S(2)}) copy-start(bf16[3,2,576,64]{2,3,1,0:T(8,128)(2,1)S(1)} %get-tuple-element.949) | copy-start | bytes 1327108 | tf_op jit(solution)/shard_map/while
  261.5 8.1 %copy-start.52 = (f32[64]{0:T(128)}, f32[64]{0:T(128)S(1)}, u32[]{:S(2)}) copy-start(f32[64]{0:T(128)S(1)} %get-tuple-element.737) | copy-start | bytes 772 | tf_op jit(solution)/shard_map/while
  261.5 18.3 %copy-start.49 = (f32[64]{0:T(128)}, f32[64]{0:T(128)S(1)}, u32[]{:S(2)}) copy-start(f32[64]{0:T(128)S(1)} %get-tuple-element.752) | copy-start | bytes 772 | tf_op jit(solution)/shard_map/while
  269.5 4.1 copy-start.30
  283.5 4.3 copy-start.12
  339.8 19.9 %copy-start.5 = (bf16[3,2,576,64]{2,3,1,0:T(8,128)(2,1)}, bf16[3,2,576,64]{2,3,1,0:T(8,128)(2,1)S(1)}, u32[]{:S(2)}) copy-start(bf16[3,2,576,64]{2,3,1,0:T(8,128)(2,1)S(1)} %get-tuple-element.949) | copy-start | bytes 1327108 | tf_op jit(solution)/shard_map/while
  341.8 8.1 %copy-start.52 = (f32[64]{0:T(128)}, f32[64]{0:T(128)S(1)}, u32[]{:S(2)}) copy-start(f32[64]{0:T(128)S(1)} %get-tuple-element.737) | copy-start | bytes 772 | tf_op jit(solution)/shard_map/while
  341.8 18.3 %copy-start.49 = (f32[64]{0:T(128)}, f32[64]{0:T(128)S(1)}, u32[]{:S(2)}) copy-start(f32[64]{0:T(128)S(1)} %get-tuple-element.752) | copy-start | bytes 772 | tf_op jit(solution)/shard_map/while
  349.7 4.1 copy-start.30
  363.7 4.3 copy-start.12
  420.1 19.9 %copy-start.5 = (bf16[3,2,576,64]{2,3,1,0:T(8,128)(2,1)}, bf16[3,2,576,64]{2,3,1,0:T(8,128)(2,1)S(1)}, u32[]{:S(2)}) copy-start(bf16[3,2,576,64]{2,3,1,0:T(8,128)(2,1)S(1)} %get-tuple-element.949) | copy-start | bytes 1327108 | tf_op jit(solution)/shard_map/while
  422.0 8.1 %copy-start.52 = (f32[64]{0:T(128)}, f32[64]{0:T(128)S(1)}, u32[]{:S(2)}) copy-start(f32[64]{0:T(128)S(1)} %get-tuple-element.737) | copy-start | bytes 772 | tf_op jit(solution)/shard_map/while
  422.0 18.3 %copy-start.49 = (f32[64]{0:T(128)}, f32[64]{0:T(128)S(1)}, u32[]{:S(2)}) copy-start(f32[64]{0:T(128)S(1)} %get-tuple-element.752) | copy-start | bytes 772 | tf_op jit(solution)/shard_map/while
  430.0 4.1 copy-start.30
  444.0 4.3 copy-start.12
  500.4 19.9 %copy-start.5 = (bf16[3,2,576,64]{2,3,1,0:T(8,128)(2,1)}, bf16[3,2,576,64]{2,3,1,0:T(8,128)(2,1)S(1)}, u32[]{:S(2)}) copy-start(bf16[3,2,576,64]{2,3,1,0:T(8,128)(2,1)S(1)} %get-tuple-element.949) | copy-start | bytes 1327108 | tf_op jit(solution)/shard_map/while
  502.3 8.1 %copy-start.52 = (f32[64]{0:T(128)}, f32[64]{0:T(128)S(1)}, u32[]{:S(2)}) copy-start(f32[64]{0:T(128)S(1)} %get-tuple-element.737) | copy-start | bytes 772 | tf_op jit(solution)/shard_map/while
  502.3 18.3 %copy-start.49 = (f32[64]{0:T(128)}, f32[64]{0:T(128)S(1)}, u32[]{:S(2)}) copy-start(f32[64]{0:T(128)S(1)} %get-tuple-element.752) | copy-start | bytes 772 | tf_op jit(solution)/shard_map/while
  524.3 4.3 copy-start.12
  580.7 19.9 %copy-start.5 = (bf16[3,2,576,64]{2,3,1,0:T(8,128)(2,1)}, bf16[3,2,576,64]{2,3,1,0:T(8,128)(2,1)S(1)}, u32[]{:S(2)}) copy-start(bf16[3,2,576,64]{2,3,1,0:T(8,128)(2,1)S(1)} %get-tuple-element.949) | copy-start | bytes 1327108 | tf_op jit(solution)/shard_map/while
  582.6 8.1 %copy-start.52 = (f32[64]{0:T(128)}, f32[64]{0:T(128)S(1)}, u32[]{:S(2)}) copy-start(f32[64]{0:T(128)S(1)} %get-tuple-element.737) | copy-start | bytes 772 | tf_op jit(solution)/shard_map/while
  582.6 18.3 %copy-start.49 = (f32[64]{0:T(128)}, f32[64]{0:T(128)S(1)}, u32[]{:S(2)}) copy-start(f32[64]{0:T(128)S(1)} %get-tuple-element.752) | copy-start | bytes 772 | tf_op jit(solution)/shard_map/while
  604.6 4.3 copy-start.12
  660.9 36.8 %copy-start.45 = (f32[3,2,2,64]{3,2,1,0:T(2,128)S(1)}, f32[3,2,2,64]{3,2,1,0:T(2,128)}, u32[]{:S(2)}) copy-start(f32[3,2,2,64]{3,2,1,0:T(2,128)} %get-tuple-element.157) | copy-start | bytes 9220
  660.9 36.8 %copy-start.56 = (f32[10]{0:T(128)S(1)}, f32[10]{0:T(128)}, u32[]{:S(2)}) copy-start(f32[10]{0:T(128)} %get-tuple-element.159) | copy-start | bytes 124
  660.9 36.8 %copy-start.62 = (f32[64,10]{0,1:T(8,128)S(1)}, f32[64,10]{0,1:T(8,128)}, u32[]{:S(2)}) copy-start(f32[64,10]{0,1:T(8,128)} %get-tuple-element.158) | copy-start | bytes 7684
  661.0 77.3 %copy-start.58 = (f32[10]{0:T(128)S(1)}, f32[10]{0:T(128)}, u32[]{:S(2)}) copy-start(f32[10]{0:T(128)} %get-tuple-element.965) | copy-start | bytes 124
  661.0 79.1 %copy-start.42 = (f32[64,10]{0,1:T(8,128)S(1)}, f32[64,10]{0,1:T(8,128)}, u32[]{:S(2)}) copy-start(f32[64,10]{0,1:T(8,128)} %get-tuple-element.963) | copy-start | bytes 7684
  661.0 118.6 %copy-start.27 = (f32[3,2,576,16]{2,3,1,0:T(8,128)S(1)}, f32[3,2,576,16]{2,3,1,0:T(8,128)}, u32[]{:S(2)}) copy-start(f32[3,2,576,16]{2,3,1,0:T(8,128)} %param.11) | copy-start | bytes 663556
  661.0 118.5 %all-reduce.57.cloned.1.call-start = ((), (), s32[]{:S(2)}) async-start(), calls=%async_computation.1 | async-start | bytes 1966080 | tf_op jit(solution)/shard_map/psum | solution.py:153
  (425 other events, 849.4 us)
Sparse Core Ops, SparseCore 0:
  661.1 36.5 all-reduce.54
  701.5 77.9 all-reduce.56
